TPU v7x, 32 devices: a whole 2x2x4 slice. The times are simulated.
32 devices in a mesh: groups: 2 (over x), fsdp: 16 (over z, y, core).
Axes of the slice: x: 2, y: 2, z: 4, core: 2. Of those that a mesh axis runs over, the one named last changes fastest.
Arguments:
- activations: bfloat16 [4096, 8192], P(('groups', 'fsdp')), parts along dimension 0, may hold values from -6 to 6
- grad_out: bfloat16 [4096, 1024], P(('groups', 'fsdp')), parts along dimension 0, may hold values from -6 to 6
- base_weight: bfloat16 [8192, 1024], P('fsdp'), may hold values from -0.1875 to 0.1875
- adapter_down: bfloat16 [16, 8192, 128], P('fsdp'), may hold values from -0.5 to 0.5
- adapter_up: bfloat16 [16, 128, 1024], P('fsdp'), may hold values from -0.5 to 0.5
- row_tenant: int32 [4096, 1], P(('groups', 'fsdp')), parts along dimension 0, may hold values from 0 to 15; in each aligned block of 128 rows (0 to 127, 128 to 255, ...) at most 16 rows name the same one
- rank_bucket: int32 [16], replicated, may hold values from 0 to 2
- owner_slot: int32 [16], replicated, may hold values from 0 to 15, each once
Outputs:
- input_gradient: bfloat16 [4096, 8192], P(('groups', 'fsdp')), parts along dimension 0
- grad_down: float32 [32, 8192, 128], P(('groups', 'fsdp')), parts along dimension 0
- grad_up: float32 [32, 128, 1024], P(('groups', 'fsdp')), parts along dimension 0
There are 2 independent parts, one for each index of `groups`. A program takes and returns all parts, laid end to end along the dimension named above; an argument that names none is the same for every part. Nothing has to cross between parts.
Inputs may be any that keep to these rules, and one draw needn't show every extreme that they name: `row_tenant`: on the rows of one device at most 16 rows belong to one tenant, and some tenant has exactly 16 there; every tenant has rows somewhere. `rank_bucket`: 0, 1 and 2 stand for ranks 8, 32 and 128. `owner_slot`: A permutation of the slots.
All inputs are finite; a program needn't handle non-finite values.
Results may differ from a plain program's by a relative error of at most 0.008.
Values may be sent and summed in bfloat16 or wider, within the bound.
A program may use at most 128 MiB of HBM per device.

v0:
```python
import jax
import jax.numpy as jnp
from jax import lax
from jax.sharding import PartitionSpec as P

MODEL_WIDTH = 8192
KV = 1024
R_SMALL = 8
R_MID = 32
RMAX = 128


adapter_alpha = 16.0


def contract_dims(left, right, left_dim, right_dim):
    return lax.dot_general(
        left, right, (((left_dim,), (right_dim,)), ((), ())), preferred_element_type=jnp.float32
    )


def masked_product(
    rank_ceiling, incoming_rows, gradient_rows, down_weight, up_weight, adapter_scale
):
    rank_mask = (jnp.arange(RMAX, dtype=jnp.int32) < rank_ceiling).astype(jnp.float32)
    hidden_state = (contract_dims(incoming_rows, down_weight, 1, 0) * rank_mask).astype(
        jnp.bfloat16
    )
    backward_rows = (contract_dims(gradient_rows, up_weight, 1, 1) * rank_mask).astype(jnp.bfloat16)
    adapter_rows = (adapter_scale * contract_dims(backward_rows, down_weight, 1, 1)).astype(
        jnp.bfloat16
    )
    down_gradient = adapter_scale * contract_dims(incoming_rows, backward_rows, 0, 0)
    up_gradient = adapter_scale * contract_dims(hidden_state, gradient_rows, 0, 0)
    return (adapter_rows, down_gradient, up_gradient)


def on_device(
    activations,
    grad_out,
    base_weight,
    adapter_down,
    adapter_up,
    row_tenant,
    rank_bucket,
    owner_slot,
):
    row_count = activations.shape[0]
    tenant_ids = rank_bucket.shape[0]
    local_slots = adapter_down.shape[0]
    device_list = lax.axis_size("fsdp")
    slot_capacity = max(2, 2 * row_count // tenant_ids)
    tenant = row_tenant[:, 0]
    onehot = (tenant[:, None] == jnp.arange(tenant_ids, dtype=jnp.int32)[None, :]).astype(jnp.int32)
    within = jnp.sum((jnp.cumsum(onehot, axis=0) - onehot) * onehot, axis=1)
    owner_index = jnp.sum(onehot * owner_slot[None, :], axis=1)
    slot_position = owner_index * slot_capacity + within
    send_in = (
        jnp.zeros((tenant_ids * slot_capacity, MODEL_WIDTH), jnp.bfloat16)
        .at[slot_position]
        .set(activations)
    )
    send_grad = (
        jnp.zeros((tenant_ids * slot_capacity, KV), jnp.bfloat16).at[slot_position].set(grad_out)
    )
    send_in = send_in.reshape(device_list, local_slots, slot_capacity, MODEL_WIDTH)
    send_grad = send_grad.reshape(device_list, local_slots, slot_capacity, KV)
    recv_in, recv_grad = (
        lax.all_to_all(send_in, "fsdp", split_axis=0, concat_axis=0, tiled=True),
        lax.all_to_all(send_grad, "fsdp", split_axis=0, concat_axis=0, tiled=True),
    )
    recv_in = jnp.transpose(recv_in, (1, 0, 2, 3)).reshape(
        local_slots, device_list * slot_capacity, MODEL_WIDTH
    )
    recv_grad = jnp.transpose(recv_grad, (1, 0, 2, 3)).reshape(
        local_slots, device_list * slot_capacity, KV
    )
    my_slots = lax.axis_index("fsdp") * local_slots + jnp.arange(local_slots, dtype=jnp.int32)
    matched = (owner_slot[None, :] == my_slots[:, None]).astype(jnp.int32)
    my_bucket = jnp.sum(matched * rank_bucket[None, :], axis=1)
    bucket_rank = jnp.where(my_bucket == 0, R_SMALL, jnp.where(my_bucket == 1, R_MID, RMAX)).astype(
        jnp.int32
    )
    bucket_scale = adapter_alpha / bucket_rank.astype(jnp.float32)
    adapter_pieces, down_pieces, up_pieces = ([], [], [])
    final_result = masked_product(
        bucket_rank[0], recv_in[0], recv_grad[0], adapter_down[0], adapter_up[0], bucket_scale[0]
    )
    adapter_pieces.append(final_result[0])
    down_pieces.append(final_result[1])
    up_pieces.append(final_result[2])
    adapter_outgoing = jnp.stack(adapter_pieces).reshape(
        local_slots, device_list, slot_capacity, MODEL_WIDTH
    )
    adapter_outgoing = jnp.transpose(adapter_outgoing, (1, 0, 2, 3))
    returned_rows = lax.all_to_all(
        adapter_outgoing, "fsdp", split_axis=0, concat_axis=0, tiled=True
    )
    adapter_term = returned_rows.reshape(tenant_ids * slot_capacity, MODEL_WIDTH)[slot_position]
    column_part = contract_dims(
        lax.all_gather(grad_out, "fsdp", axis=0, tiled=True), base_weight, 1, 1
    ).astype(jnp.bfloat16)
    frozen_term = lax.all_to_all(column_part, "fsdp", split_axis=0, concat_axis=1, tiled=True)
    input_gradient = (frozen_term.astype(jnp.float32) + adapter_term.astype(jnp.float32)).astype(
        jnp.bfloat16
    )
    return (input_gradient, jnp.stack(down_pieces), jnp.stack(up_pieces))


def solution(mesh):
    placed = (
        P(("groups", "fsdp"), None),
        P(("groups", "fsdp"), None),
        P("fsdp", None),
        P("fsdp", None, None),
        P("fsdp", None, None),
        P(("groups", "fsdp"), None),
        P(),
        P(),
    )
    return jax.shard_map(
        on_device,
        mesh=mesh,
        in_specs=placed,
        out_specs=(
            P(("groups", "fsdp"), None),
            P(("groups", "fsdp"), None, None),
            P(("groups", "fsdp"), None, None),
        ),
        check_vma=False,
    )
```

profile of v0, /device:TPU:29, one launch (start us, length us, event | category | flops | bytes accessed | tf_op | source)
XLA Modules:
  0.0 315.8 jit_solution(12050988444335076622)
XLA Ops:
  7.2 0.9 fusion.21
  8.2 0.8 select_reduce_fusion.1
  9.1 2.4 scatter_custom_fusion
  11.5 6.3 %all-to-all-start.1 = ((bf16[16,1,16,1024]{3,2,1,0:T(8,128)(2,1)}), bf16[16,1,16,1024]{3,2,1,0:T(8,128)(2,1)S(1)}, u32[]{:S(2)}, u32[]{:S(2)}) async-start(bf16[16,1,16,1024]{3,2,1,0:T(8,128)(2,1)} %bitcast.6), calls=%async_computation.1 | async-start | bytes 1048576 | tf_op jit(solution)/shard_map/all_to_all | solution.py:70
  17.8 7.0 %scatter_custom_fusion.1 = bf16[256,8192]{1,0:T(8,128)(2,1)} fusion(s32[128]{0:T(128)S(1)} %fusion.23, bf16[128,8192]{1,0:T(8,128)(2,1)} %param.8, bf16[]{:T(256)} %constant.36.clone.1), kind=kCustom, calls=%fused_computation.13 | custom fusion | bytes 4194816 | tf_op jit(solution)/shard_map/scatter | solution.py:61
  24.8 5.7 %all-to-all-done.1 = bf16[16,1,16,1024]{3,2,1,0:T(8,128)(2,1)S(1)} async-done(((bf16[16,1,16,1024]{3,2,1,0:T(8,128)(2,1)}), bf16[16,1,16,1024]{3,2,1,0:T(8,128)(2,1)S(1)}, u32[]{:S(2)}, u32[]{:S(2)}) %all-to-all-start.1) | async-done | bytes 524320 | tf_op jit(solution)/shard_map/all_to_all | solution.py:70
  30.5 6.3 %all-to-all-start.3 = ((bf16[16,1,16,8192]{3,2,1,0:T(8,128)(2,1)}), bf16[16,1,16,8192]{3,2,1,0:T(8,128)(2,1)}, u32[]{:S(2)}, u32[]{:S(2)}) async-start(bf16[16,1,16,8192]{3,2,1,0:T(8,128)(2,1)} %bitcast.48), calls=%async_computation.3 | async-start | bytes 8388608 | tf_op jit(solution)/shard_map/all_to_all | solution.py:69
  36.9 0.7 all-gather.2.cloned.1.call-update
  37.6 0.6 fusion.22
  39.6 0.3 fusion.11
  39.9 3.3 %fusion = bf16[256,8192]{1,0:T(8,128)(2,1)} fusion(bf16[256,128]{1,0:T(8,128)(2,1)S(1)} %fusion.11, f32[]{:T(128)S(6)} %div.4, bf16[1,8192,128]{2,1,0:T(8,128)(2,1)S(1)} %copy-done), kind=kOutput, calls=%fused_computation.4 | convolution fusion | flops 541065216 | bytes 6356996 | tf_op jit(solution)/shard_map/dot_general | solution.py:17
  43.2 110.4 %all-to-all-done.3 = bf16[16,1,16,8192]{3,2,1,0:T(8,128)(2,1)} async-done(((bf16[16,1,16,8192]{3,2,1,0:T(8,128)(2,1)}), bf16[16,1,16,8192]{3,2,1,0:T(8,128)(2,1)}, u32[]{:S(2)}, u32[]{:S(2)}) %all-to-all-start.3) | async-done | bytes 4194336 | tf_op jit(solution)/shard_map/all_to_all | solution.py:69
  153.6 5.9 %all-to-all-start.2 = ((bf16[16,1,16,8192]{3,2,1,0:T(8,128)(2,1)}), bf16[16,1,16,8192]{3,2,1,0:T(8,128)(2,1)}, u32[]{:S(2)}, u32[]{:S(2)}) async-start(bf16[16,1,16,8192]{3,2,1,0:T(8,128)(2,1)} %bitcast.49), calls=%async_computation.2 | async-start | bytes 8388608 | tf_op jit(solution)/shard_map/all_to_all | solution.py:96
  159.5 6.2 %convolution_convert_fusion = bf16[2048,512]{1,0:T(8,128)(2,1)} fusion(bf16[2048,1024]{1,0:T(8,128)(2,1)} %all-gather.2.cloned.1.call-done, bf16[512,1024]{1,0:T(8,128)(2,1)} %param.10), kind=kOutput, calls=%fused_computation.9 | convolution fusion | flops 2148532224 | bytes 7340032 | tf_op jit(solution)/shard_map/dot_general | solution.py:17
  165.7 85.3 %all-to-all-done.2 = bf16[16,1,16,8192]{3,2,1,0:T(8,128)(2,1)} async-done(((bf16[16,1,16,8192]{3,2,1,0:T(8,128)(2,1)}), bf16[16,1,16,8192]{3,2,1,0:T(8,128)(2,1)}, u32[]{:S(2)}, u32[]{:S(2)}) %all-to-all-start.2) | async-done | bytes 4194336 | tf_op jit(solution)/shard_map/all_to_all | solution.py:96
  251.0 5.9 %all-to-all-start = ((bf16[16,128,512]{2,1,0:T(8,128)(2,1)}), bf16[16,128,512]{2,1,0:T(8,128)(2,1)}, u32[]{:S(2)}, u32[]{:S(2)}) async-start(bf16[16,128,512]{2,1,0:T(8,128)(2,1)} %bitcast.53), calls=%async_computation | async-start | bytes 4194304 | tf_op jit(solution)/shard_map/all_to_all | solution.py:103
  256.8 5.5 %fusion.1 = f32[1,8192,128]{2,1,0:T(8,128)} fusion(bf16[256,8192]{1,0:T(8,128)(2,1)} %bitcast.15, bf16[256,128]{1,0:T(8,128)(2,1)S(1)} %fusion.11, f32[]{:T(128)S(6)} %div.4), kind=kOutput, calls=%fused_computation.6 | convolution fusion | flops 537919488 | bytes 8454148 | tf_op jit(solution)/shard_map/dot_general | solution.py:17
  262.4 4.5 %fusion.7 = f32[1,128,1024]{2,1,0:T(8,128)} fusion(bf16[256,1024]{1,0:T(8,128)(2,1)S(1)} %bitcast.52, bf16[256,8192]{1,0:T(8,128)(2,1)} %bitcast.15, bf16[1,8192,128]{2,1,0:T(8,128)(2,1)S(1)} %copy-done, f32[]{:T(128)S(6)} %div.4, f32[128]{0:T(128)S(1)} %compare_convert_fusion), kind=kOutput, calls=%fused_computation.16 | convolution fusion | flops 604176384 | bytes 7340548 | tf_op jit(solution)/shard_map/dot_general | solution.py:17
  266.8 7.8 %gather_fusion = bf16[128,8192]{1,0:T(8,128)(2,1)} fusion(bf16[256,8192]{1,0:T(8,128)(2,1)} %bitcast.12, s32[1024]{0:T(1024)S(1)} %pad_clamp_fusion), kind=kCustom, calls=%fused_computation | custom fusion | bytes 4194816 | tf_op jit(solution)/shard_map/gather | solution.py:99
  274.7 28.7 %all-to-all-done = bf16[16,128,512]{2,1,0:T(8,128)(2,1)} async-done(((bf16[16,128,512]{2,1,0:T(8,128)(2,1)}), bf16[16,128,512]{2,1,0:T(8,128)(2,1)}, u32[]{:S(2)}, u32[]{:S(2)}) %all-to-all-start) | async-done | bytes 2097184 | tf_op jit(solution)/shard_map/all_to_all | solution.py:103
  303.4 2.1 convert_bitcast_fusion
  305.6 0.5 copy.17
  306.1 1.1 copy-done.1
  307.2 1.8 add_convert_fusion
  (15 shorter events, 0.3 us)
Async XLA Ops:
  7.2 32.8 %copy-start = (bf16[1,8192,128]{2,1,0:T(8,128)(2,1)S(1)}, bf16[1,8192,128]{2,1,0:T(8,128)(2,1)}, u32[]{:S(2)}) copy-start(bf16[1,8192,128]{2,1,0:T(8,128)(2,1)} %param.11) | copy-start | bytes 6291460
  11.5 19.0 %all-to-all-start.1 = ((bf16[16,1,16,1024]{3,2,1,0:T(8,128)(2,1)}), bf16[16,1,16,1024]{3,2,1,0:T(8,128)(2,1)S(1)}, u32[]{:S(2)}, u32[]{:S(2)}) async-start(bf16[16,1,16,1024]{3,2,1,0:T(8,128)(2,1)} %bitcast.6), calls=%async_computation.1 | async-start | bytes 1048576 | tf_op jit(solution)/shard_map/all_to_all | solution.py:70
  30.5 7.1 %copy-start.3 = (s32[16]{0:T(128)S(1)}, s32[16]{0:T(128)}, u32[]{:S(2)}) copy-start(s32[16]{0:T(128)} %param.15) | copy-start | bytes 196
  30.5 7.1 %copy-start.4 = (s32[16]{0:T(128)S(1)}, s32[16]{0:T(128)}, u32[]{:S(2)}) copy-start(s32[16]{0:T(128)} %param.14) | copy-start | bytes 196
  30.5 9.1 %copy-start.2 = (bf16[1,128,1024]{2,1,0:T(8,128)(2,1)S(1)}, bf16[1,128,1024]{2,1,0:T(8,128)(2,1)}, u32[]{:S(2)}) copy-start(bf16[1,128,1024]{2,1,0:T(8,128)(2,1)} %param.12) | copy-start | bytes 786436
  30.5 123.1 %all-to-all-start.3 = ((bf16[16,1,16,8192]{3,2,1,0:T(8,128)(2,1)}), bf16[16,1,16,8192]{3,2,1,0:T(8,128)(2,1)}, u32[]{:S(2)}, u32[]{:S(2)}) async-start(bf16[16,1,16,8192]{3,2,1,0:T(8,128)(2,1)} %bitcast.48), calls=%async_computation.3 | async-start | bytes 8388608 | tf_op jit(solution)/shard_map/all_to_all | solution.py:69
  36.9 122.6 %all-gather.2.cloned.1.call-start = ((), (), s32[]{:S(2)}) async-start(), calls=%async_computation.4 | async-start | bytes 4456448 | tf_op jit(solution)/shard_map/all_gather | solution.py:101
  153.6 97.4 %all-to-all-start.2 = ((bf16[16,1,16,8192]{3,2,1,0:T(8,128)(2,1)}), bf16[16,1,16,8192]{3,2,1,0:T(8,128)(2,1)}, u32[]{:S(2)}, u32[]{:S(2)}) async-start(bf16[16,1,16,8192]{3,2,1,0:T(8,128)(2,1)} %bitcast.49), calls=%async_computation.2 | async-start | bytes 8388608 | tf_op jit(solution)/shard_map/all_to_all | solution.py:96
  251.0 52.4 %all-to-all-start = ((bf16[16,128,512]{2,1,0:T(8,128)(2,1)}), bf16[16,128,512]{2,1,0:T(8,128)(2,1)}, u32[]{:S(2)}, u32[]{:S(2)}) async-start(bf16[16,128,512]{2,1,0:T(8,128)(2,1)} %bitcast.53), calls=%async_computation | async-start | bytes 4194304 | tf_op jit(solution)/shard_map/all_to_all | solution.py:103
  305.6 1.6 copy-start.1
Sparse Core Ops, SparseCore 0:
  39.9 96.3 all-gather.1
where the time goes:
time: 318 us; the launch traced here: 316 us
  waiting for transfers between devices  231 us (73%)
  starting transfers between devices  24.4 us (8%)
  matrix products  19.8 us (6%)
  local copies, waits for them, and re-layouts  18.8 us (6%)
  between operations  15.5 us (5%)
  other arithmetic  6.5 us (2%)
    all_to_all x1, waiting for transfers between devices, on_device(): lax.all_to_all(send_in, 'fsdp', split_axis=0, concat_axis=0, tiled=True)  110 us
    all_to_all x1, waiting for transfers between devices, on_device(): lax.all_to_all(adapter_outgoing, 'fsdp', split_axis=0, concat_axis=0, til...  85.3 us
    all_to_all x1, waiting for transfers between devices, on_device(): lax.all_to_all(column_part, 'fsdp', split_axis=0, concat_axis=1, tiled=True)  28.7 us
    dot_general x5, matrix products, contract_dims(): lax.dot_general(left, right, (((left_dim,), (right_dim,)), ((), ())), pre...  19.8 us
    gather x1, local copies, waits for them, and re-layouts, on_device(): returned_rows.reshape(tenant_ids * slot_capacity, MODEL_WIDTH)  7.83 us
    scatter x1, local copies, waits for them, and re-layouts, on_device(): send_in = jnp.zeros((tenant_ids * slot_capacity, MODEL_WIDTH), jnp.bfloat...  7.01 us
  transfers between devices with their start and end apart: 5, of which 4 were waited for; matrix products, arithmetic and copies ran while one was open for 11% of the time, Pallas kernels for 0%

commit v1 on v0

v1 whole, which is shorter than its diff:
```python
import jax
import jax.numpy as jnp
from jax import lax
from jax.sharding import PartitionSpec as P

R_SMALL = 8
R_MID = 32
RMAX = 128
ALPHA = 16.0


def dot(a, b, dims, batch=((), ())):
    return lax.dot_general(a, b, (dims, batch), preferred_element_type=jnp.float32)


def on_device(
    activations,
    grad_out,
    base_weight,
    adapter_down,
    adapter_up,
    row_tenant,
    rank_bucket,
    owner_slot,
):
    bf16 = jnp.bfloat16
    rows, width = activations.shape
    kv = grad_out.shape[1]
    tenants = rank_bucket.shape[0]
    n = lax.axis_size("fsdp")
    groups = lax.axis_size("groups")
    me = lax.axis_index("fsdp")
    my_group = lax.axis_index("groups")
    cap = max(2, 2 * rows // tenants)
    cols = width // n
    part = cols // groups
    down, up = adapter_down[0], adapter_up[0]

    my_part = lax.dynamic_index_in_dim(
        down.reshape(n, groups, part, RMAX), my_group, axis=1, keepdims=False
    )
    parts = lax.all_to_all(my_part, "fsdp", split_axis=0, concat_axis=0, tiled=True)
    slices = lax.all_gather(parts, "groups", axis=1, tiled=True)

    grad_all = lax.all_gather(grad_out, "fsdp", axis=0, tiled=True).reshape(n, rows, kv)
    tenant = lax.all_gather(row_tenant[:, 0], "fsdp", axis=0, tiled=True).reshape(n, rows)

    same = tenant[:, :, None] == tenant[:, None, :]
    before = jnp.arange(rows)[None, :, None] > jnp.arange(rows)[None, None, :]
    within = jnp.sum((same & before).astype(jnp.int32), axis=2)
    hot = tenant[:, :, None] == jnp.arange(tenants, dtype=jnp.int32)
    slot = jnp.sum(jnp.where(hot, owner_slot, 0), axis=2)
    place = slot * cap + within
    perm = (
        place[:, None, :] == jnp.arange(tenants * cap, dtype=jnp.int32)[None, :, None]
    ).astype(bf16)
    perm_mine = lax.dynamic_index_in_dim(perm, me, axis=0, keepdims=False)
    pick = lax.dynamic_slice_in_dim(perm, me * cap, cap, axis=1)

    bucket_of_slot = jnp.sum(
        jnp.where(owner_slot[None, :] == jnp.arange(tenants)[:, None], rank_bucket[None, :], 0),
        axis=1,
    )
    ranks = jnp.where(bucket_of_slot == 0, R_SMALL, jnp.where(bucket_of_slot == 1, R_MID, RMAX))
    scales = ALPHA / ranks.astype(jnp.float32)
    my_rank, my_scale = ranks[me], scales[me]
    mask = (jnp.arange(RMAX, dtype=jnp.int32) < my_rank).astype(jnp.float32)

    sent = dot(perm_mine, activations, ((1,), (0,))).astype(bf16)
    came = lax.all_to_all(
        sent.reshape(n, cap, width), "fsdp", split_axis=0, concat_axis=0, tiled=True
    ).reshape(n * cap, width)

    grads = dot(pick, grad_all, ((2,), (1,)), ((0,), (0,))).astype(bf16).reshape(n * cap, kv)
    back = (dot(grads, up, ((1,), (1,))) * mask).astype(bf16)
    backs = lax.all_gather(back, "fsdp", axis=0, tiled=True).reshape(tenants, n * cap, RMAX)

    lora = dot(backs, slices, ((2,), (2,)), ((0,), (0,))) * scales[:, None, None]
    lora = lora.astype(bf16).reshape(tenants, n, cap, cols)
    lora = jnp.transpose(lora, (1, 0, 2, 3)).reshape(n, tenants * cap, cols)
    lora = dot(perm, lora, ((1,), (1,)), ((0,), (0,)))
    base = dot(grad_all.reshape(n * rows, kv), base_weight, ((1,), (1,))).astype(bf16)
    total = (base.reshape(n, rows, cols).astype(jnp.float32) + lora).astype(bf16)
    input_gradient = lax.all_to_all(
        total.reshape(n * rows, cols), "fsdp", split_axis=0, concat_axis=1, tiled=True
    )

    hidden = (dot(came, down, ((1,), (0,))) * mask).astype(bf16)
    grad_down = my_scale * dot(came, back, ((0,), (0,)))
    grad_up = my_scale * dot(hidden, grads, ((0,), (0,)))
    return input_gradient, grad_down[None], grad_up[None]


def solution(mesh):
    rows = P(("groups", "fsdp"), None)
    return jax.shard_map(
        on_device,
        mesh=mesh,
        in_specs=(
            rows,
            rows,
            P("fsdp", None),
            P("fsdp", None, None),
            P("fsdp", None, None),
            rows,
            P(),
            P(),
        ),
        out_specs=(
            rows,
            P(("groups", "fsdp"), None, None),
            P(("groups", "fsdp"), None, None),
        ),
        check_vma=False,
    )
```

time: 318 us -> 245 us (0.77)
  waiting for transfers between devices: 231 us -> 117 us
  blocking collectives: 0 us -> 41.9 us
  matrix products: 19.8 us -> 30.5 us
  other arithmetic: 6.5 us -> 1.84 us
  local copies, waits for them, and re-layouts: 18.8 us -> 14.9 us
    all_to_all x4 -> x3, waiting for transfers between devices: 230 us -> 34 us  [the longest x1 34 us: on_device(): lax.all_to_all(total.reshape(n * rows, cols), 'fsdp', split_axis=0, conca...]
    all_gather x1 -> x3, waiting for transfers between devices: 0.01 us -> 81.6 us  [the longest x1 56.6 us: on_device(): lax.all_gather(back, 'fsdp', axis=0, tiled=True)]
    all_gather x0 -> x1, blocking collectives: none -> 41.9 us  [on_device(): lax.all_gather(row_tenant[:, 0], 'fsdp', axis=0, tiled=True)]
    dot_general x5 -> x8, matrix products: 19.8 us -> 30.5 us  [dot(): lax.dot_general(a, b, (dims, batch), preferred_element_type=jnp.float32)]
    scatter x2 -> x0, local copies, waits for them, and re-layouts: 9.38 us -> none  [the longest x1 7.01 us: on_device(): send_in = jnp.zeros((tenant_ids * slot_capacity, MODEL_WIDTH), jnp.bfloat...]
    gather x1 -> x0, local copies, waits for them, and re-layouts: 7.83 us -> none  [on_device(): returned_rows.reshape(tenant_ids * slot_capacity, MODEL_WIDTH)]
    unnamed x10 -> x19, local copies, waits for them, and re-layouts: 1.12 us -> 6.8 us
    all_to_all x0 -> x1, local copies, waits for them, and re-layouts: none -> 3.94 us  [on_device(): lax.all_to_all(total.reshape(n * rows, cols), 'fsdp', split_axis=0, conca...]
  transfers between devices with their start and end apart: 5 -> 6, of which waited for: 4 -> 3; matrix products, arithmetic and copies ran while one was open for 11% -> 15% of each run, Pallas kernels for 0% -> 0%
where the time goes in v1:
time: 245 us; the launch traced here: 244 us
  waiting for transfers between devices  117 us (48%)
  blocking collectives  41.9 us (17%)
  matrix products  30.5 us (12%)
  starting transfers between devices  23.6 us (10%)
  local copies, waits for them, and re-layouts  14.9 us (6%)
  between operations  13.9 us (6%)
    all_gather x1, waiting for transfers between devices, on_device(): lax.all_gather(back, 'fsdp', axis=0, tiled=True)  56.6 us
    all_gather x1, blocking collectives, on_device(): lax.all_gather(row_tenant[:, 0], 'fsdp', axis=0, tiled=True)  41.9 us
    all_to_all x1, waiting for transfers between devices, on_device(): lax.all_to_all(total.reshape(n * rows, cols), 'fsdp', split_axis=0, conca...  34 us
    dot_general x8, matrix products, dot(): lax.dot_general(a, b, (dims, batch), preferred_element_type=jnp.float32)  30.5 us
    all_gather x1, waiting for transfers between devices, on_device(): slices = lax.all_gather(parts, 'groups', axis=1, tiled=True)  25 us
    all_to_all x1, starting transfers between devices, on_device(): lax.all_to_all(total.reshape(n * rows, cols), 'fsdp', split_axis=0, conca...  11.2 us
    unnamed x19, local copies, waits for them, and re-layouts  6.8 us
    all_to_all x1, starting transfers between devices, on_device(): lax.all_to_all(my_part, 'fsdp', split_axis=0, concat_axis=0, tiled=True)  6.33 us
  transfers between devices with their start and end apart: 6, of which 3 were waited for; matrix products, arithmetic and copies ran while one was open for 15% of the time, Pallas kernels for 0%

profile of v1, /device:TPU:29, one launch (start us, length us, event | category | flops | bytes accessed | tf_op | source)
XLA Modules:
  0.0 243.6 jit_solution(1270752091968652216)
XLA Ops:
  7.2 0.7 all-gather.5.cloned.1.call-update
  7.9 2.3 dynamic-slice_bitcast_fusion
  10.2 6.3 %all-to-all-start = ((bf16[16,256,128]{2,1,0:T(8,128)(2,1)}), bf16[16,256,128]{2,1,0:T(8,128)(2,1)S(1)}, u32[]{:S(2)}, u32[]{:S(2)}) async-start(bf16[16,256,128]{2,1,0:T(8,128)(2,1)} %dynamic-slice_bitcast_fusion), calls=%async_computation | async-start | bytes 2097152 | tf_op jit(solution)/shard_map/all_to_all | solution.py:42
  16.6 41.9 %all-gather = s32[2048,1]{0,1:T(1,128)S(1)} all-gather(s32[128,1]{0,1:T(1,128)S(1)} %copy-done.6), channel_id=2, replica_groups=mesh['groups'=2,'fsdp'=16] {'fsdp'}, dimensions={0}, use_global_device_ids=true | all-gather | bytes 8704 | tf_op jit(solution)/shard_map/all_gather | solution.py:46
  59.6 0.8 copy-done.3
  60.4 3.2 %convolution_convert_fusion = bf16[256,8192]{1,0:T(8,128)(2,1)} fusion(bf16[128,8192]{1,0:T(8,128)(2,1)S(1)} %copy-done, pred[16,256,128]{2,1,0:T(8,128)(4,1)S(1)} %iota_compare_fusion, s32[]{:T(128)S(6)} %select_n.42), kind=kOutput, calls=%fused_computation | convolution fusion | flops 538968064 | bytes 6324228 | tf_op jit(solution)/shard_map/dot_general | solution.py:13
  63.7 1.0 copy-done.1
  64.6 5.9 %all-to-all-start.2 = ((bf16[16,16,8192]{2,1,0:T(8,128)(2,1)}), bf16[16,16,8192]{2,1,0:T(8,128)(2,1)}, u32[]{:S(2)}, u32[]{:S(2)}) async-start(bf16[16,16,8192]{2,1,0:T(8,128)(2,1)} %bitcast.53), calls=%async_computation.2 | async-start | bytes 8388608 | tf_op jit(solution)/shard_map/all_to_all | solution.py:70
  70.6 0.7 all-gather.9.cloned.1.call-update
  72.0 0.6 compare_convert_fusion
  72.7 2.9 %convolution_convert_fusion.2 = bf16[16,16,1024]{2,1,0:T(8,128)(2,1)S(1)} fusion(bf16[16,128,1024]{2,1,0:T(8,128)(2,1)} %bitcast.59, pred[16,256,128]{2,1,0:T(8,128)(4,1)} %copy-done.3, s32[]{:T(128)S(6)} %select_n.38), kind=kOutput, calls=%fused_computation.10 | convolution fusion | flops 67371008 | bytes 4751364 | tf_op jit(solution)/shard_map/dot_general | solution.py:13
  75.6 0.9 fusion.8
  76.6 6.2 %convolution_convert_fusion.1 = bf16[2048,512]{1,0:T(8,128)(2,1)} fusion(bf16[2048,1024]{1,0:T(8,128)(2,1)} %all-gather.5.cloned.1.call-done, bf16[512,1024]{1,0:T(8,128)(2,1)} %param.10), kind=kOutput, calls=%fused_computation.6 | convolution fusion | flops 2148532224 | bytes 7340032 | tf_op jit(solution)/shard_map/dot_general | solution.py:13
  82.8 25.0 %all-gather.9.cloned.1.call-done = bf16[16,512,128]{2,1,0:T(8,128)(2,1)} async-done(((bf16[16,256,128]{2,1,0:T(8,128)(2,1)}), bf16[16,512,128]{2,1,0:T(8,128)(2,1)}) %all-gather.9.cloned.1.call-update) | async-done | bytes 2097168 | tf_op jit(solution)/shard_map/all_gather | solution.py:43
  107.7 56.6 %all-gather.7.cloned.1.call-done = bf16[4096,128]{1,0:T(8,128)(2,1)} async-done(((bf16[256,128]{1,0:T(8,128)(2,1)}), bf16[4096,128]{1,0:T(8,128)(2,1)}) %all-gather.7.cloned.1.call-update) | async-done | bytes 1048592 | tf_op jit(solution)/shard_map/all_gather | solution.py:76
  164.3 3.2 %multiply_convert_fusion = bf16[16,256,512]{2,1,0:T(8,128)(2,1)S(1)} fusion(f32[16]{0:T(128)S(1)} %get-tuple-element.9, bf16[16,256,128]{2,1,0:T(8,128)(2,1)} %bitcast.61, bf16[16,512,128]{2,1,0:T(8,128)(2,1)} %all-gather.9.cloned.1.call-done), kind=kOutput, calls=%fused_computation.3 | convolution fusion | flops 541065216 | bytes 7340096 | tf_op jit(solution)/shard_map/dot_general | solution.py:13
  168.2 0.9 copy-done.2
  169.1 2.2 fusion.1
  171.3 11.2 %all-to-all-start.1 = ((bf16[16,128,512]{2,1,0:T(8,128)(2,1)}), bf16[16,128,512]{2,1,0:T(8,128)(2,1)}, u32[]{:S(2)}, u32[]{:S(2)}) async-start(bf16[16,128,512]{2,1,0:T(8,128)(2,1)} %fusion.1), calls=%async_computation.1 | async-start | bytes 4194304 | tf_op jit(solution)/shard_map/all_to_all | solution.py:84
  183.2 6.1 %fusion = f32[1,8192,128]{2,1,0:T(8,128)} fusion(bf16[256,8192]{1,0:T(8,128)(2,1)} %bitcast.17, bf16[256,128]{1,0:T(8,128)(2,1)S(1)} %copy-done.4, f32[]{:T(128)} %bitcast.14), kind=kOutput, calls=%fused_computation.2 | convolution fusion | flops 537919488 | bytes 8454148 | tf_op jit(solution)/shard_map/dot_general | solution.py:13
  189.3 5.8 %fusion.4 = f32[1,128,1024]{2,1,0:T(8,128)} fusion(bf16[256,1024]{1,0:T(8,128)(2,1)S(1)} %bitcast.58, bf16[256,8192]{1,0:T(8,128)(2,1)} %bitcast.17, bf16[1,8192,128]{2,1,0:T(8,128)(2,1)} %param.11, f32[]{:T(128)} %bitcast.14, f32[128]{0:T(128)S(1)} %compare_convert_fusion), kind=kOutput, calls=%fused_computation.12 | convolution fusion | flops 604176384 | bytes 7340548 | tf_op jit(solution)/shard_map/dot_general | solution.py:13
  195.1 34.0 %all-to-all-done.1 = bf16[16,128,512]{2,1,0:T(8,128)(2,1)} async-done(((bf16[16,128,512]{2,1,0:T(8,128)(2,1)}), bf16[16,128,512]{2,1,0:T(8,128)(2,1)}, u32[]{:S(2)}, u32[]{:S(2)}) %all-to-all-start.1) | async-done | bytes 2097184 | tf_op jit(solution)/shard_map/all_to_all | solution.py:84
  229.1 3.9 %copy.22 = bf16[128,16,512]{0,2,1:T(8,128)(2,1)} copy(bf16[128,16,512]{2,0,1:T(8,128)(2,1)} %bitcast.12) | data formatting | bytes 4194304 | tf_op jit(solution)/shard_map/all_to_all | solution.py:84
  233.0 4.1 %copy.23 = bf16[128,8192]{1,0:T(8,128)(2,1)} copy(bf16[128,8192]{0,1:T(8,128)(2,1)} %bitcast.55) | data formatting | bytes 4194304
  (32 shorter events, 3.3 us)
Async XLA Ops:
  7.2 53.2 %copy-start = (bf16[128,8192]{1,0:T(8,128)(2,1)S(1)}, bf16[128,8192]{1,0:T(8,128)(2,1)}, u32[]{:S(2)}) copy-start(bf16[128,8192]{1,0:T(8,128)(2,1)} %param.8) | copy-start | bytes 6291460
  7.2 9.4 %copy-start.6 = (s32[128,1]{0,1:T(1,128)S(1)}, s32[128,1]{0,1:T(1,128)}, u32[]{:S(2)}) copy-start(s32[128,1]{0,1:T(1,128)} %param.13) | copy-start | bytes 1540
  7.2 51.3 %copy-start.7 = (s32[16]{0:T(128)S(1)}, s32[16]{0:T(128)}, u32[]{:S(2)}) copy-start(s32[16]{0:T(128)} %param.15) | copy-start | bytes 196
  7.2 65.5 %all-gather.5.cloned.1.call-start = ((), (), s32[]{:S(2)}) async-start(), calls=%async_computation.3 | async-start | bytes 4456448 | tf_op jit(solution)/shard_map/all_gather | solution.py:45
  10.2 53.4 %all-to-all-start = ((bf16[16,256,128]{2,1,0:T(8,128)(2,1)}), bf16[16,256,128]{2,1,0:T(8,128)(2,1)S(1)}, u32[]{:S(2)}, u32[]{:S(2)}) async-start(bf16[16,256,128]{2,1,0:T(8,128)(2,1)} %dynamic-slice_bitcast_fusion), calls=%async_computation | async-start | bytes 2097152 | tf_op jit(solution)/shard_map/all_to_all | solution.py:42
  59.6 0.8 copy-start.3
  63.7 1.0 copy-start.1
  63.7 7.7 %copy-start.8 = (s32[16]{0:T(128)S(1)}, s32[16]{0:T(128)}, u32[]{:S(2)}) copy-start(s32[16]{0:T(128)} %param.14) | copy-start | bytes 196
  64.6 106.7 %all-to-all-start.2 = ((bf16[16,16,8192]{2,1,0:T(8,128)(2,1)}), bf16[16,16,8192]{2,1,0:T(8,128)(2,1)}, u32[]{:S(2)}, u32[]{:S(2)}) async-start(bf16[16,16,8192]{2,1,0:T(8,128)(2,1)} %bitcast.53), calls=%async_computation.2 | async-start | bytes 8388608 | tf_op jit(solution)/shard_map/all_to_all | solution.py:70
  70.5 5.1 %copy-start.5 = (bf16[1,128,1024]{2,1,0:T(8,128)(2,1)S(1)}, bf16[1,128,1024]{2,1,0:T(8,128)(2,1)}, u32[]{:S(2)}) copy-start(bf16[1,128,1024]{2,1,0:T(8,128)(2,1)} %param.12) | copy-start | bytes 786436
  70.5 37.2 %all-gather.9.cloned.1.call-start = ((), (), s32[]{:S(2)}) async-start(), calls=%async_computation.5 | async-start | bytes 3145728 | tf_op jit(solution)/shard_map/all_gather | solution.py:43
  71.3 93.1 %all-gather.7.cloned.1.call-start = ((), (), s32[]{:S(2)}) async-start(), calls=%async_computation.4 | async-start | bytes 1114112 | tf_op jit(solution)/shard_map/all_gather | solution.py:76
  167.5 1.6 copy-start.2
  171.3 11.9 %copy-start.4 = (bf16[256,128]{1,0:T(8,128)(2,1)S(1)}, bf16[256,128]{1,0:T(8,128)(2,1)}, u32[]{:S(2)}) copy-start(bf16[256,128]{1,0:T(8,128)(2,1)} %fusion.8) | copy-start | bytes 196612
  171.3 57.8 %all-to-all-start.1 = ((bf16[16,128,512]{2,1,0:T(8,128)(2,1)}), bf16[16,128,512]{2,1,0:T(8,128)(2,1)}, u32[]{:S(2)}, u32[]{:S(2)}) async-start(bf16[16,128,512]{2,1,0:T(8,128)(2,1)} %fusion.1), calls=%async_computation.1 | async-start | bytes 4194304 | tf_op jit(solution)/shard_map/all_to_all | solution.py:84
Sparse Core Ops, SparseCore 0:
  10.2 62.2 all-gather.4
  74.1 33.6 all-gather.8
  110.5 53.8 all-gather.6

commit v2 on v1

--- a/solution.py
+++ b/solution.py
@@ -1,6 +1,10 @@
+import functools
+
 import jax
 import jax.numpy as jnp
 from jax import lax
+from jax.experimental import pallas as pl
+from jax.experimental.pallas import tpu as pltpu
 from jax.sharding import PartitionSpec as P
 
 R_SMALL = 8
@@ -11,6 +15,336 @@
 
 def dot(a, b, dims, batch=((), ())):
     return lax.dot_general(a, b, (dims, batch), preferred_element_type=jnp.float32)
+
+
+MESH = pl.DeviceIdType.MESH
+
+
+def exchange_kernel(
+    n,
+    groups,
+    pack_ref,
+    sent_ref,
+    down_ref,
+    up_ref,
+    weight_ref,
+    mask_ref,
+    my_scale_ref,
+    scales_ref,
+    out_ref,
+    grad_down_ref,
+    grad_up_ref,
+    packs,
+    came,
+    slices,
+    backs,
+    grads,
+    lora,
+    total,
+    pack_send,
+    pack_recv,
+    back_send,
+    back_recv,
+    down_send,
+    down_recv,
+    x_send,
+    x_recv,
+    act_send,
+    act_recv,
+    out_send,
+    out_recv,
+    local_sem,
+):
+    bf16 = jnp.bfloat16
+    me = lax.axis_index("fsdp")
+    group = lax.axis_index("groups")
+    cap, width = sent_ref.shape[1], sent_ref.shape[2]
+    rows = pack_ref.shape[0]
+    kv = grads.shape[2]
+    cols = slices.shape[1]
+    part = cols // groups
+    w = me % 4
+    across = me - w + (w + 2) % 4
+    beside = me + 1 - 2 * (w % 2)
+    line = n // 4
+
+    def remote(src, dst, send, recv, to, to_group=None):
+        return pltpu.make_async_remote_copy(
+            src_ref=src,
+            dst_ref=dst,
+            send_sem=send,
+            recv_sem=recv,
+            device_id=(group if to_group is None else to_group, to),
+            device_id_type=MESH,
+        )
+
+    def peer(k):
+        return lax.rem(me + k, n)
+
+    def source(k):
+        return lax.rem(me + n - k, n)
+
+    def loop(first, last, body):
+        lax.fori_loop(first, last, lambda k, c: (body(k), c)[1], 0)
+
+    barrier = pltpu.get_barrier_semaphore()
+    loop(1, n, lambda k: pl.semaphore_signal(
+        barrier, inc=1, device_id=(group, peer(k)), device_id_type=MESH))
+    for d in range(1, groups):
+        pl.semaphore_signal(
+            barrier, inc=1, device_id=((group + d) % groups, me), device_id_type=MESH)
+
+    packs[me] = pack_ref[...]
+    keep = pltpu.make_async_copy(sent_ref.at[me], came.at[me], local_sem)
+    keep.start()
+    slices[me] = down_ref[pl.ds(pl.multiple_of(me * cols, cols), cols), :]
+    pl.semaphore_wait(barrier, n - 1 + groups - 1)
+
+    def gather_start(buf, send, recv):
+        own = buf.at[me]
+        for k in range(1, line):
+            remote(own, own, send.at[k], recv.at[k], peer(4 * k)).start()
+        remote(own, own, send.at[line], recv.at[line], across).start()
+        remote(own, own, send.at[2 * line], recv.at[2 * line], beside).start()
+
+    def gather_finish(buf, send, recv):
+        def copy_b(i, k):
+            return remote(buf.at[i], buf.at[i], send.at[line + k], recv.at[line + k], across)
+
+        def copy_c(i, k):
+            at = 2 * line + k
+            return remote(buf.at[i], buf.at[i], send.at[at], recv.at[at], beside)
+
+        def from_line(origin, k):
+            return lax.rem(origin + n - 4 * k, n)
+
+        for k in range(1, line):
+            i = source(4 * k)
+            remote(buf.at[i], buf.at[i], send.at[k], recv.at[k], peer(4 * k)).wait_recv()
+            copy_b(i, k).start()
+            copy_c(i, k).start()
+        for k in range(line):
+            i = from_line(across, k)
+            copy_b(i, k).wait_recv()
+            copy_c(i, line + k).start()
+        other = beside - beside % 4 + (beside % 4 + 2) % 4
+        for k in range(line):
+            copy_c(from_line(beside, k), k).wait_recv()
+        for k in range(line):
+            copy_c(from_line(other, k), line + k).wait_recv()
+
+    def gather_sent(buf, send, recv):
+        for k in range(1, 4 * line):
+            remote(buf.at[me], buf.at[me], send.at[k], recv.at[k], beside).wait_send()
+
+    def down_part(k):
+        j = peer(k)
+        start = pl.multiple_of(j * cols + group * part, part)
+        return remote(
+            down_ref.at[pl.ds(start, part), :],
+            slices.at[me, pl.ds(pl.multiple_of(group * part, part), part), :],
+            down_send.at[k], down_recv.at[k], j)
+
+    def place_of(k, owner):
+        return slices.at[source(k), pl.ds(pl.multiple_of(owner * part, part), part), :]
+
+    gather_start(packs, pack_send, pack_recv)
+    loop(1, n, lambda k: down_part(k).start())
+    gather_finish(packs, pack_send, pack_recv)
+
+    def act(k):
+        j = peer(k)
+        return remote(sent_ref.at[j], came.at[me], act_send.at[k], act_recv.at[k], j)
+
+    wanted = (
+        lax.broadcasted_iota(jnp.int32, (n * cap, cap), 0)
+        == lax.broadcasted_iota(jnp.int32, (n * cap, cap), 1) + me * cap
+    ).astype(bf16)
+
+    def pick(b):
+        chosen = dot(packs[b, :, kv:], wanted, ((1,), (0,))).astype(bf16)
+        grads[b] = dot(chosen, packs[b, :, :kv], ((0,), (0,))).astype(bf16)
+
+    loop(0, n, pick)
+    back = dot(grads[...].reshape(n * cap, kv), up_ref[...], ((1,), (1,))) * mask_ref[...]
+    backs[me] = back.astype(bf16)
+    gather_start(backs, back_send, back_recv)
+
+    def relay(k):
+        remote(place_of(k, group), place_of(k, group), down_send.at[k], down_recv.at[k],
+               peer(k)).wait_recv()
+        for d in range(1, groups):
+            remote(place_of(k, group), place_of(k, group), x_send.at[d, k], x_recv.at[d, k],
+                   me, (group + d) % groups).start()
+
+    loop(1, n, relay)
+    gather_finish(backs, back_send, back_recv)
+    loop(1, n, lambda k: act(k).start())
+
+    def base(b):
+        total[b] = dot(packs[b, :, :kv], weight_ref[...], ((1,), (1,))).astype(bf16)
+
+    loop(0, n, base)
+
+    def relayed(k):
+        for d in range(1, groups):
+            spot = place_of(k, (group + groups - d) % groups)
+            remote(spot, spot, x_send.at[d, k], x_recv.at[d, k], me,
+                   (group + d) % groups).wait_recv()
+
+    loop(1, n, relayed)
+
+    def low_rank(t):
+        term = dot(backs[t], slices[t], ((1,), (1,))) * scales_ref[t]
+        lora[:, t] = term.astype(bf16).reshape(n, cap, cols)
+
+    loop(0, n, low_rank)
+
+    def combine(b):
+        term = dot(packs[b, :, kv:], lora[b].reshape(n * cap, cols), ((1,), (0,)))
+        total[b] = (total[b].astype(jnp.float32) + term).astype(bf16)
+
+    def columns(i):
+        return out_ref.at[:, pl.ds(pl.multiple_of(i * cols, cols), cols)]
+
+    def result(k):
+        j = peer(k)
+        return remote(total.at[j], columns(me), out_send.at[k], out_recv.at[k], j)
+
+    def combine_and_send(k):
+        combine(peer(k))
+        result(k).start()
+
+    loop(1, n, combine_and_send)
+    combine(me)
+    out_ref[:, pl.ds(pl.multiple_of(me * cols, cols), cols)] = total[me]
+
+    def arrived(k):
+        spot = came.at[source(k)]
+        remote(spot, spot, act_send.at[k], act_recv.at[k], peer(k)).wait_recv()
+
+    loop(1, n, arrived)
+    keep.wait()
+    my_back = backs[me]
+    chunk = 1024
+    hidden = jnp.zeros((n * cap, RMAX), jnp.float32)
+    for c in range(width // chunk):
+        at = pl.ds(c * chunk, chunk)
+        held = came[:, :, at].reshape(n * cap, chunk)
+        hidden += dot(held, down_ref[at, :], ((1,), (0,)))
+        grad_down_ref[at, :] = dot(held, my_back, ((0,), (0,))) * my_scale_ref[...]
+    hidden = (hidden * mask_ref[...]).astype(bf16)
+    up_scale = my_scale_ref[0:1, 0:1]
+    grad_up_ref[...] = (
+        dot(hidden, grads[...].reshape(n * cap, kv), ((0,), (0,))) * up_scale
+    )
+
+    def received(k):
+        spot = columns(source(k))
+        remote(total.at[me], spot, out_send.at[k], out_recv.at[k], peer(k)).wait_recv()
+
+    loop(1, n, received)
+    gather_sent(packs, pack_send, pack_recv)
+    gather_sent(backs, back_send, back_recv)
+
+    def all_sent(k):
+        down_part(k).wait_send()
+        for d in range(1, groups):
+            remote(place_of(k, group), place_of(k, group), x_send.at[d, k], x_recv.at[d, k],
+                   me, (group + d) % groups).wait_send()
+        act(k).wait_send()
+        result(k).wait_send()
+
+    loop(1, n, all_sent)
+
+
+def one_kernel(
+    activations,
+    grad_out,
+    base_weight,
+    adapter_down,
+    adapter_up,
+    row_tenant,
+    rank_bucket,
+    owner_slot,
+):
+    bf16, f32 = jnp.bfloat16, jnp.float32
+    rows, width = activations.shape
+    kv = grad_out.shape[1]
+    tenants = rank_bucket.shape[0]
+    n = lax.axis_size("fsdp")
+    groups = lax.axis_size("groups")
+    me = lax.axis_index("fsdp")
+    cap = 2 * rows // tenants
+    cols = width // n
+
+    tenant = row_tenant[:, 0]
+    same = tenant[:, None] == tenant[None, :]
+    before = jnp.arange(rows)[:, None] > jnp.arange(rows)[None, :]
+    within = jnp.sum((same & before).astype(jnp.int32), axis=1)
+    hot = tenant[:, None] == jnp.arange(tenants, dtype=jnp.int32)
+    place = jnp.sum(jnp.where(hot, owner_slot, 0), axis=1) * cap + within
+    perm = (place[:, None] == jnp.arange(n * cap, dtype=jnp.int32)[None, :]).astype(bf16)
+    bucket_of_slot = jnp.sum(
+        jnp.where(owner_slot[None, :] == jnp.arange(tenants)[:, None], rank_bucket[None, :], 0),
+        axis=1,
+    )
+    ranks = jnp.where(bucket_of_slot == 0, R_SMALL, jnp.where(bucket_of_slot == 1, R_MID, RMAX))
+    scales = ALPHA / ranks.astype(f32)
+    mine = jnp.arange(tenants, dtype=jnp.int32) == me
+    my_rank = jnp.sum(jnp.where(mine, ranks, 0))
+    my_scale = jnp.sum(jnp.where(mine, scales, 0.0))
+    mask = (jnp.arange(RMAX, dtype=jnp.int32) < my_rank).astype(f32)[None, :]
+    sent = dot(perm, activations, ((0,), (0,))).astype(bf16).reshape(n, cap, width)
+    pack = jnp.concatenate([grad_out, perm], axis=1)
+
+    vmem = pl.BlockSpec(memory_space=pltpu.VMEM)
+    dma = pltpu.SemaphoreType.DMA
+    out, grad_down, grad_up = pl.pallas_call(
+        functools.partial(exchange_kernel, n, groups),
+        out_shape=(
+            jax.ShapeDtypeStruct((rows, width), bf16),
+            jax.ShapeDtypeStruct((width, RMAX), f32),
+            jax.ShapeDtypeStruct((RMAX, kv), f32),
+        ),
+        in_specs=[vmem, pl.BlockSpec(memory_space=pl.ANY)] + [vmem] * 6,
+        out_specs=(vmem, vmem, vmem),
+        scratch_shapes=[
+            pltpu.VMEM((n, rows, kv + n * cap), bf16),
+            pltpu.VMEM((n, cap, width), bf16),
+            pltpu.VMEM((n, cols, RMAX), bf16),
+            pltpu.VMEM((n, n * cap, RMAX), bf16),
+            pltpu.VMEM((n, cap, kv), bf16),
+            pltpu.VMEM((n, n, cap, cols), bf16),
+            pltpu.VMEM((n, rows, cols), bf16),
+            dma((n,)),
+            dma((n,)),
+            dma((n,)),
+            dma((n,)),
+            dma((n,)),
+            dma((n,)),
+            dma((groups, n)),
+            dma((groups, n)),
+            dma((n,)),
+            dma((n,)),
+            dma((n,)),
+            dma((n,)),
+            dma,
+        ],
+        compiler_params=pltpu.CompilerParams(
+            collective_id=0, has_side_effects=True, vmem_limit_bytes=56 * 1024 * 1024
+        ),
+    )(
+        pack,
+        sent,
+        adapter_down[0],
+        adapter_up[0],
+        base_weight,
+        mask,
+        jnp.broadcast_to(my_scale, (1, RMAX)),
+        jnp.broadcast_to(scales[:, None, None], (tenants, 1, cols)),
+    )
+    return out, grad_down[None], grad_up[None]
 
 
 def on_device(
@@ -93,8 +427,17 @@
 
 def solution(mesh):
     rows = P(("groups", "fsdp"), None)
-    return jax.shard_map(
-        on_device,
+    devices = mesh.shape["groups"] * mesh.shape["fsdp"]
+
+    def call(*args):
+        tokens = args[0].shape[0] // devices
+        tenants = args[6].shape[0]
+        cap = 2 * tokens // tenants
+        fits = cap % 16 == 0 and mesh.shape["fsdp"] % 4 == 0 and tenants == mesh.shape["fsdp"]
+        return mapped(one_kernel if fits else on_device)(*args)
+
+    mapped = lambda body: jax.shard_map(
+        body,
         mesh=mesh,
         in_specs=(
             rows,
@@ -113,3 +456,4 @@
         ),
         check_vma=False,
     )
+    return call

time: 245 us -> 237 us (0.967)
  Pallas kernels: 0 us -> 218 us
  waiting for transfers between devices: 117 us -> 0 us
  blocking collectives: 41.9 us -> 0 us
  matrix products: 30.5 us -> 3.37 us
  starting transfers between devices: 23.6 us -> 0 us
  between operations: 13.9 us -> 0.68 us
  local copies, waits for them, and re-layouts: 14.9 us -> 7.92 us
  other arithmetic: 1.84 us -> 6.87 us
    pallas_call x0 -> x1, Pallas kernels: none -> 218 us  [one_kernel(): pl.pallas_call(functools.partial(exchange_kernel, n, groups), out_shape=(...]
    all_gather x3 -> x0, waiting for transfers between devices: 81.6 us -> none  [the longest x1 56.6 us: on_device(): lax.all_gather(back, 'fsdp', axis=0, tiled=True)]
    all_gather x1 -> x0, blocking collectives: 41.9 us -> none  [on_device(): lax.all_gather(row_tenant[:, 0], 'fsdp', axis=0, tiled=True)]
    all_to_all x3 -> x0, waiting for transfers between devices: 34 us -> none  [the longest x1 34 us: on_device(): lax.all_to_all(total.reshape(n * rows, cols), 'fsdp', split_axis=0, conca...]
    dot_general x8 -> x1, matrix products: 30.5 us -> 3.37 us  [dot(): lax.dot_general(a, b, (dims, batch), preferred_element_type=jnp.float32)]
    all_to_all x3 -> x0, starting transfers between devices: 23.4 us -> none  [the longest x1 11.2 us: on_device(): lax.all_to_all(total.reshape(n * rows, cols), 'fsdp', split_axis=0, conca...]
    all_to_all x1 -> x0, local copies, waits for them, and re-layouts: 3.94 us -> none  [on_device(): lax.all_to_all(total.reshape(n * rows, cols), 'fsdp', split_axis=0, conca...]
    reduce_sum x3 -> x5, other arithmetic: 0.85 us -> 3.84 us  [the longest x1 0.93 us: one_kernel(): jnp.sum(jnp.where(owner_slot[None, :] == jnp.arange(tenants)[:, None], ra...]
  transfers between devices with their start and end apart: 6 -> 0, of which waited for: 3 -> 0; matrix products, arithmetic and copies ran while one was open for 15% -> 0% of each run, Pallas kernels for 0% -> 0%
where the time goes in v2:
time: 237 us
  Pallas kernels  218 us (92%)
  local copies, waits for them, and re-layouts  7.92 us (3%)
  other arithmetic  6.87 us (3%)
  matrix products  3.37 us (1%)
    pallas_call x1, Pallas kernels, one_kernel(): pl.pallas_call(functools.partial(exchange_kernel, n, groups), out_shape=(...  218 us
    unnamed x9, local copies, waits for them, and re-layouts  6.07 us

profile of v2, /device:TPU:29, one launch (start us, length us, event | category | flops | bytes accessed | tf_op | source)
XLA Modules:
  0.0 237.0 jit_solution(3567299355055015340)
XLA Ops:
  0.6 0.0 copy-start
  0.6 0.9 select_reduce_fusion
  1.6 0.6 fusion.3
  2.2 1.2 compare_convert_fusion.mask_ref
  3.5 0.6 fusion.4
  4.1 1.2 broadcast_in_dim.70.my_scale_ref
  5.2 0.9 convert_reduce_fusion
  6.1 0.8 select_reduce_fusion.1
  6.9 0.7 broadcast_in_dim.71.scales_ref
  7.6 0.1 fusion
  7.7 1.7 pad_maximum_fusion.pack_ref
  9.4 0.0 copy-done
  9.4 3.4 %convolution_convert_fusion = bf16[256,8192]{1,0:T(8,128)(2,1)} fusion(bf16[128,8192]{1,0:T(8,128)(2,1)S(1)} %copy-done, s32[128]{0:T(128)S(1)} %multiply_add_fusion), kind=kOutput, calls=%fused_computation | convolution fusion | flops 539000832 | bytes 6291968 | tf_op jit(solution)/shard_map/dot_general | solution.py:17
  12.8 218.1 %shard_map.103 = (bf16[128,8192]{1,0:T(8,128)(2,1)}, f32[8192,128]{1,0:T(8,128)}, f32[128,1024]{1,0:T(8,128)}) custom-call(bf16[128,1280]{1,0:T(8,128)(2,1)} %pad_maximum_fusion.pack_ref, bf16[16,16,8192]{2,1,0:T(8,128)(2,1)} %bitcast.7, bf16[8192,128]{1,0:T(8,128)(2,1)} %bitcast.9, bf16[128,1024]{1,0:T(8,128)(2,1)} %bitcast.11, ...), custom_call_target="tpu_custom_call" | custom-call | tf_op jit(solution)/shard_map/pallas_call | solution.py:303
  230.9 0.0 copy-start.1
  230.9 3.2 %copy.14 = bf16[128,8192]{1,0:T(8,128)(2,1)} copy(bf16[128,8192]{1,0:T(8,128)(2,1)} %get-tuple-element.14) | data formatting | bytes 4194304
  234.2 0.0 copy-done.1
  234.2 0.0 copy-start.2
  234.2 2.0 copy.15
  236.2 0.0 copy-done.2
  236.2 0.8 copy.16
  (1 shorter events, 0.0 us)
Async XLA Ops:
  0.6 8.8 %copy-start = (bf16[128,8192]{1,0:T(8,128)(2,1)S(1)}, bf16[128,8192]{1,0:T(8,128)(2,1)}, u32[]{:S(2)}) copy-start(bf16[128,8192]{1,0:T(8,128)(2,1)} %param.8) | copy-start | bytes 6291460
  230.9 3.3 %copy-start.1 = (f32[8192,128]{1,0:T(8,128)S(1)}, f32[8192,128]{1,0:T(8,128)}, u32[]{:S(2)}) copy-start(f32[8192,128]{1,0:T(8,128)} %get-tuple-element.7) | copy-start | bytes 12582916
  234.2 2.0 copy-start.2

commit v3 on v2

--- a/solution.py
+++ b/solution.py
@@ -18,13 +18,14 @@
 
 
 MESH = pl.DeviceIdType.MESH
+PIECES = 4
 
 
 def exchange_kernel(
     n,
     groups,
     pack_ref,
-    sent_ref,
+    rows_ref,
     down_ref,
     up_ref,
     weight_ref,
@@ -41,6 +42,7 @@
     grads,
     lora,
     total,
+    sent_ref,
     pack_send,
     pack_recv,
     back_send,
@@ -53,7 +55,6 @@
     act_recv,
     out_send,
     out_recv,
-    local_sem,
 ):
     bf16 = jnp.bfloat16
     me = lax.axis_index("fsdp")
@@ -95,47 +96,50 @@
             barrier, inc=1, device_id=((group + d) % groups, me), device_id_type=MESH)
 
     packs[me] = pack_ref[...]
-    keep = pltpu.make_async_copy(sent_ref.at[me], came.at[me], local_sem)
-    keep.start()
     slices[me] = down_ref[pl.ds(pl.multiple_of(me * cols, cols), cols), :]
     pl.semaphore_wait(barrier, n - 1 + groups - 1)
 
-    def gather_start(buf, send, recv):
-        own = buf.at[me]
-        for k in range(1, line):
-            remote(own, own, send.at[k], recv.at[k], peer(4 * k)).start()
-        remote(own, own, send.at[line], recv.at[line], across).start()
-        remote(own, own, send.at[2 * line], recv.at[2 * line], beside).start()
-
-    def gather_finish(buf, send, recv):
-        def copy_b(i, k):
-            return remote(buf.at[i], buf.at[i], send.at[line + k], recv.at[line + k], across)
-
-        def copy_c(i, k):
-            at = 2 * line + k
-            return remote(buf.at[i], buf.at[i], send.at[at], recv.at[at], beside)
+    def hop(buf, send, recv, pieces, i, number, p, to):
+        size = buf.shape[1] // pieces
+        spot = buf.at[i, pl.ds(p * size, size), :]
+        return remote(spot, spot, send.at[p, number], recv.at[p, number], to)
+
+    def gather_start(buf, send, recv, pieces):
+        for p in range(pieces):
+            for k in range(1, line):
+                hop(buf, send, recv, pieces, me, k, p, peer(4 * k)).start()
+            hop(buf, send, recv, pieces, me, line, p, across).start()
+            hop(buf, send, recv, pieces, me, 2 * line, p, beside).start()
+
+    def gather_finish(buf, send, recv, pieces):
+        def copy(i, number, p, to):
+            return hop(buf, send, recv, pieces, i, number, p, to)
 
         def from_line(origin, k):
             return lax.rem(origin + n - 4 * k, n)
 
-        for k in range(1, line):
-            i = source(4 * k)
-            remote(buf.at[i], buf.at[i], send.at[k], recv.at[k], peer(4 * k)).wait_recv()
-            copy_b(i, k).start()
-            copy_c(i, k).start()
-        for k in range(line):
-            i = from_line(across, k)
-            copy_b(i, k).wait_recv()
-            copy_c(i, line + k).start()
         other = beside - beside % 4 + (beside % 4 + 2) % 4
-        for k in range(line):
-            copy_c(from_line(beside, k), k).wait_recv()
-        for k in range(line):
-            copy_c(from_line(other, k), line + k).wait_recv()
-
-    def gather_sent(buf, send, recv):
-        for k in range(1, 4 * line):
-            remote(buf.at[me], buf.at[me], send.at[k], recv.at[k], beside).wait_send()
+        for p in range(pieces):
+            for k in range(1, line):
+                i = source(4 * k)
+                copy(i, k, p, peer(4 * k)).wait_recv()
+                copy(i, line + k, p, across).start()
+                copy(i, 2 * line + k, p, beside).start()
+        for p in range(pieces):
+            for k in range(line):
+                i = from_line(across, k)
+                copy(i, line + k, p, across).wait_recv()
+                copy(i, 3 * line + k, p, beside).start()
+        for p in range(pieces):
+            for k in range(line):
+                copy(from_line(beside, k), 2 * line + k, p, beside).wait_recv()
+            for k in range(line):
+                copy(from_line(other, k), 3 * line + k, p, beside).wait_recv()
+
+    def gather_sent(buf, send, recv, pieces):
+        for p in range(pieces):
+            for k in range(1, 4 * line):
+                hop(buf, send, recv, pieces, me, k, p, beside).wait_send()
 
     def down_part(k):
         j = peer(k)
@@ -148,9 +152,16 @@
     def place_of(k, owner):
         return slices.at[source(k), pl.ds(pl.multiple_of(owner * part, part), part), :]
 
-    gather_start(packs, pack_send, pack_recv)
+    gather_start(packs, pack_send, pack_recv, PIECES)
     loop(1, n, lambda k: down_part(k).start())
-    gather_finish(packs, pack_send, pack_recv)
+
+    def order_rows(c):
+        at = pl.ds(pl.multiple_of(c * 1024, 1024), 1024)
+        moved = dot(pack_ref[:, kv:], rows_ref[:, at], ((0,), (0,))).astype(bf16)
+        sent_ref[:, :, at] = moved.reshape(n, cap, 1024)
+
+    loop(0, width // 1024, order_rows)
+    gather_finish(packs, pack_send, pack_recv, PIECES)
 
     def act(k):
         j = peer(k)
@@ -168,7 +179,9 @@
     loop(0, n, pick)
     back = dot(grads[...].reshape(n * cap, kv), up_ref[...], ((1,), (1,))) * mask_ref[...]
     backs[me] = back.astype(bf16)
-    gather_start(backs, back_send, back_recv)
+    gather_start(backs, back_send, back_recv, 1)
+
+    loop(1, n, lambda k: act(k).start())
 
     def relay(k):
         remote(place_of(k, group), place_of(k, group), down_send.at[k], down_recv.at[k],
@@ -178,13 +191,15 @@
                    me, (group + d) % groups).start()
 
     loop(1, n, relay)
-    gather_finish(backs, back_send, back_recv)
-    loop(1, n, lambda k: act(k).start())
-
-    def base(b):
-        total[b] = dot(packs[b, :, :kv], weight_ref[...], ((1,), (1,))).astype(bf16)
-
-    loop(0, n, base)
+    gather_finish(backs, back_send, back_recv, 1)
+
+    def base(i):
+        some = pl.ds(i * 4, 4)
+        block = packs[some, :, :kv].reshape(4 * rows, kv)
+        product = dot(block, weight_ref[...], ((1,), (1,))).astype(bf16)
+        total[some] = product.reshape(4, rows, cols)
+
+    loop(0, line, base)
 
     def relayed(k):
         for d in range(1, groups):
@@ -224,7 +239,7 @@
         remote(spot, spot, act_send.at[k], act_recv.at[k], peer(k)).wait_recv()
 
     loop(1, n, arrived)
-    keep.wait()
+    came[me] = sent_ref[me]
     my_back = backs[me]
     chunk = 1024
     hidden = jnp.zeros((n * cap, RMAX), jnp.float32)
@@ -244,8 +259,8 @@
         remote(total.at[me], spot, out_send.at[k], out_recv.at[k], peer(k)).wait_recv()
 
     loop(1, n, received)
-    gather_sent(packs, pack_send, pack_recv)
-    gather_sent(backs, back_send, back_recv)
+    gather_sent(packs, pack_send, pack_recv, PIECES)
+    gather_sent(backs, back_send, back_recv, 1)
 
     def all_sent(k):
         down_part(k).wait_send()
@@ -295,7 +310,6 @@
     my_rank = jnp.sum(jnp.where(mine, ranks, 0))
     my_scale = jnp.sum(jnp.where(mine, scales, 0.0))
     mask = (jnp.arange(RMAX, dtype=jnp.int32) < my_rank).astype(f32)[None, :]
-    sent = dot(perm, activations, ((0,), (0,))).astype(bf16).reshape(n, cap, width)
     pack = jnp.concatenate([grad_out, perm], axis=1)
 
     vmem = pl.BlockSpec(memory_space=pltpu.VMEM)
@@ -307,7 +321,7 @@
             jax.ShapeDtypeStruct((width, RMAX), f32),
             jax.ShapeDtypeStruct((RMAX, kv), f32),
         ),
-        in_specs=[vmem, pl.BlockSpec(memory_space=pl.ANY)] + [vmem] * 6,
+        in_specs=[vmem] * 8,
         out_specs=(vmem, vmem, vmem),
         scratch_shapes=[
             pltpu.VMEM((n, rows, kv + n * cap), bf16),
@@ -317,10 +331,11 @@
             pltpu.VMEM((n, cap, kv), bf16),
             pltpu.VMEM((n, n, cap, cols), bf16),
             pltpu.VMEM((n, rows, cols), bf16),
-            dma((n,)),
-            dma((n,)),
-            dma((n,)),
-            dma((n,)),
+            pltpu.VMEM((n, cap, width), bf16),
+            dma((PIECES, n)),
+            dma((PIECES, n)),
+            dma((1, n)),
+            dma((1, n)),
             dma((n,)),
             dma((n,)),
             dma((groups, n)),
@@ -329,14 +344,13 @@
             dma((n,)),
             dma((n,)),
             dma((n,)),
-            dma,
         ],
         compiler_params=pltpu.CompilerParams(
             collective_id=0, has_side_effects=True, vmem_limit_bytes=56 * 1024 * 1024
         ),
     )(
         pack,
-        sent,
+        activations,
         adapter_down[0],
         adapter_up[0],
         base_weight,

time: 237 us -> 222 us (0.937)
  Pallas kernels: 218 us -> 207 us
  matrix products: 3.37 us -> 0 us
    pallas_call x1, Pallas kernels: 218 us -> 207 us  [one_kernel(): pl.pallas_call(functools.partial(exchange_kernel, n, groups), out_shape=(...]
    dot_general x1 -> x0, matrix products: 3.37 us -> none  [dot(): lax.dot_general(a, b, (dims, batch), preferred_element_type=jnp.float32)]
    unnamed x9 -> x7, local copies, waits for them, and re-layouts: 6.07 us -> 6.06 us
where the time goes in v3:
time: 222 us
  Pallas kernels  207 us (93%)
  local copies, waits for them, and re-layouts  8 us (4%)
  other arithmetic  6.64 us (3%)
    pallas_call x1, Pallas kernels, one_kernel(): pl.pallas_call(functools.partial(exchange_kernel, n, groups), out_shape=(...  207 us
    unnamed x7, local copies, waits for them, and re-layouts  6.06 us

profile of v3, /device:TPU:29, one launch (start us, length us, event | category | flops | bytes accessed | tf_op | source)
XLA Modules:
  0.0 221.9 jit_solution(6398747764334514617)
XLA Ops:
  0.6 0.8 select_reduce_fusion
  1.4 0.6 fusion.2
  2.1 1.2 compare_convert_fusion.mask_ref
  3.2 0.6 fusion.3
  3.8 1.2 broadcast_in_dim.70.my_scale_ref
  5.1 0.9 convert_reduce_fusion
  6.0 0.8 select_reduce_fusion.1
  6.7 0.7 broadcast_in_dim.71.scales_ref
  7.4 0.1 fusion
  7.5 1.7 pad_maximum_fusion.pack_ref
  9.2 206.6 %shard_map.103 = (bf16[128,8192]{1,0:T(8,128)(2,1)}, f32[8192,128]{1,0:T(8,128)}, f32[128,1024]{1,0:T(8,128)}) custom-call(bf16[128,1280]{1,0:T(8,128)(2,1)} %pad_maximum_fusion.pack_ref, bf16[128,8192]{1,0:T(8,128)(2,1)} %rows_ref.1, bf16[8192,128]{1,0:T(8,128)(2,1)} %bitcast.6, bf16[128,1024]{1,0:T(8,128)(2,1)} %bitcast.8, bf16[512,1024]{1,0:T(8,128)(2,1)} %weight_ref.1, ...), custom_call_target="tpu_custom_call" | custom-call | tf_op jit(solution)/shard_map/pallas_call | solution.py:317
  215.8 0.0 copy-start
  215.8 3.2 %copy.14 = bf16[128,8192]{1,0:T(8,128)(2,1)} copy(bf16[128,8192]{1,0:T(8,128)(2,1)} %get-tuple-element.14) | data formatting | bytes 4194304
  219.1 0.0 copy-done
  219.1 0.0 copy-start.1
  219.1 2.0 copy.15
  221.1 0.0 copy-done.1
  221.1 0.8 copy.16
  (1 shorter events, 0.0 us)
Async XLA Ops:
  215.8 3.3 %copy-start = (f32[8192,128]{1,0:T(8,128)S(1)}, f32[8192,128]{1,0:T(8,128)}, u32[]{:S(2)}) copy-start(f32[8192,128]{1,0:T(8,128)} %get-tuple-element.7) | copy-start | bytes 12582916
  219.1 2.0 copy-start.1

commit v4 on v3

--- a/solution.py
+++ b/solution.py
@@ -167,22 +167,6 @@
         j = peer(k)
         return remote(sent_ref.at[j], came.at[me], act_send.at[k], act_recv.at[k], j)
 
-    wanted = (
-        lax.broadcasted_iota(jnp.int32, (n * cap, cap), 0)
-        == lax.broadcasted_iota(jnp.int32, (n * cap, cap), 1) + me * cap
-    ).astype(bf16)
-
-    def pick(b):
-        chosen = dot(packs[b, :, kv:], wanted, ((1,), (0,))).astype(bf16)
-        grads[b] = dot(chosen, packs[b, :, :kv], ((0,), (0,))).astype(bf16)
-
-    loop(0, n, pick)
-    back = dot(grads[...].reshape(n * cap, kv), up_ref[...], ((1,), (1,))) * mask_ref[...]
-    backs[me] = back.astype(bf16)
-    gather_start(backs, back_send, back_recv, 1)
-
-    loop(1, n, lambda k: act(k).start())
-
     def relay(k):
         remote(place_of(k, group), place_of(k, group), down_send.at[k], down_recv.at[k],
                peer(k)).wait_recv()
@@ -191,6 +175,23 @@
                    me, (group + d) % groups).start()
 
     loop(1, n, relay)
+
+    wanted = (
+        lax.broadcasted_iota(jnp.int32, (n * cap, cap), 0)
+        == lax.broadcasted_iota(jnp.int32, (n * cap, cap), 1) + me * cap
+    ).astype(bf16)
+
+    def pick(b):
+        chosen = dot(packs[b, :, kv:], wanted, ((1,), (0,))).astype(bf16)
+        grads[b] = dot(chosen, packs[b, :, :kv], ((0,), (0,))).astype(bf16)
+
+    loop(0, n, pick)
+    back = dot(grads[...].reshape(n * cap, kv), up_ref[...], ((1,), (1,))) * mask_ref[...]
+    backs[me] = back.astype(bf16)
+    gather_start(backs, back_send, back_recv, 1)
+
+    loop(1, n, lambda k: act(k).start())
+
     gather_finish(backs, back_send, back_recv, 1)
 
     def base(i):

time: 222 us -> 227 us (1.023)
  Pallas kernels: 207 us -> 211 us
    pallas_call x1, Pallas kernels: 207 us -> 211 us  [one_kernel(): pl.pallas_call(functools.partial(exchange_kernel, n, groups), out_shape=(...]
where the time goes in v4:
time: 227 us
  Pallas kernels  211 us (93%)
  local copies, waits for them, and re-layouts  8 us (4%)
  other arithmetic  6.64 us (3%)
    pallas_call x1, Pallas kernels, one_kernel(): pl.pallas_call(functools.partial(exchange_kernel, n, groups), out_shape=(...  211 us
    unnamed x7, local copies, waits for them, and re-layouts  6.06 us

profile of v4, /device:TPU:29, one launch (start us, length us, event | category | flops | bytes accessed | tf_op | source)
XLA Modules:
  0.0 226.7 jit_solution(62592051859305188)
XLA Ops:
  0.6 0.8 select_reduce_fusion
  1.4 0.6 fusion.2
  2.1 1.2 compare_convert_fusion.mask_ref
  3.2 0.6 fusion.3
  3.8 1.2 broadcast_in_dim.70.my_scale_ref
  5.1 0.9 convert_reduce_fusion
  6.0 0.8 select_reduce_fusion.1
  6.7 0.7 broadcast_in_dim.71.scales_ref
  7.4 0.1 fusion
  7.5 1.7 pad_maximum_fusion.pack_ref
  9.2 211.3 %shard_map.103 = (bf16[128,8192]{1,0:T(8,128)(2,1)}, f32[8192,128]{1,0:T(8,128)}, f32[128,1024]{1,0:T(8,128)}) custom-call(bf16[128,1280]{1,0:T(8,128)(2,1)} %pad_maximum_fusion.pack_ref, bf16[128,8192]{1,0:T(8,128)(2,1)} %rows_ref.1, bf16[8192,128]{1,0:T(8,128)(2,1)} %bitcast.6, bf16[128,1024]{1,0:T(8,128)(2,1)} %bitcast.8, bf16[512,1024]{1,0:T(8,128)(2,1)} %weight_ref.1, ...), custom_call_target="tpu_custom_call" | custom-call | tf_op jit(solution)/shard_map/pallas_call | solution.py:318
  220.6 0.0 copy-start
  220.6 3.2 %copy.14 = bf16[128,8192]{1,0:T(8,128)(2,1)} copy(bf16[128,8192]{1,0:T(8,128)(2,1)} %get-tuple-element.14) | data formatting | bytes 4194304
  223.8 0.0 copy-done
  223.8 0.0 copy-start.1
  223.8 2.0 copy.15
  225.9 0.0 copy-done.1
  225.9 0.8 copy.16
  (1 shorter events, 0.0 us)
Async XLA Ops:
  220.6 3.3 %copy-start = (f32[8192,128]{1,0:T(8,128)S(1)}, f32[8192,128]{1,0:T(8,128)}, u32[]{:S(2)}) copy-start(f32[8192,128]{1,0:T(8,128)} %get-tuple-element.7) | copy-start | bytes 12582916
  223.8 2.0 copy-start.1
